TPU v7x, 32 devices: a whole 2x2x4 slice. The times are simulated.
32 devices in a mesh: lat: 8 (over y, x, core), lon: 4 (over z).
Axes of the slice: x: 2, y: 2, z: 4, core: 2. Of those that a mesh axis runs over, the one named last changes fastest.
Arguments:
- grid_state: bfloat16 [120, 192, 128], P('lat', 'lon'), may hold values from -6 to 6
- weight_in: bfloat16 [6, 128, 384], replicated, may hold values from -0.5 to 0.5
- bias_in: float32 [6, 384], replicated, may hold values from -4 to 4
- weight_out: bfloat16 [6, 384, 128], replicated, may hold values from -0.3125 to 0.3125
- quad_weights: float32 [120], replicated, may hold values from 0.5 to 2
- diffusion: float32 [128], replicated, may hold values from 0.3 to 30
- legendre: bfloat16 [32, 120, 32], P('lon'), may hold values from -0.5 to 0.5
- chan_table: int32 [128], replicated, may hold values from 0 to 127, each once
- wave_table: int32 [32], replicated, may hold values from 0 to 31, each once
Outputs:
- updated: bfloat16 [120, 192, 128], P('lat', 'lon')
- spectral: float32 [32, 128, 2, 32], P('lon', 'lat')
Inputs may be any that keep to these rules, and one draw needn't show every extreme that they name: `chan_table`: each channel 0 to 127 stands exactly once. `wave_table`: each wavenumber 0 to 31 stands exactly once.
All inputs are finite; a program needn't handle non-finite values.
Results may differ from a plain program's by a relative error of at most 0.012.
Values may be sent and summed in bfloat16 or wider, within the bound.
A program may use at most 64 MiB of HBM per device.

v0:
```python
import math
import jax
import jax.numpy as jnp
from jax import lax
from jax.sharding import PartitionSpec as P


def column_layers(column_rows, weight_in, bias_in, weight_out):
    hidden_state = column_rows.astype(jnp.float32)
    for layer_idx in range(weight_in.shape[0]):
        inv_rms = lax.rsqrt(jnp.mean(hidden_state * hidden_state, axis=-1, keepdims=True) + 1e-06)
        normed = (hidden_state * inv_rms).astype(jnp.bfloat16)
        pre_act = (
            jnp.dot(normed, weight_in[layer_idx], preferred_element_type=jnp.float32)
            + bias_in[layer_idx]
        )
        activation = jax.nn.gelu(pre_act, approximate=True).astype(jnp.bfloat16)
        hidden_state = hidden_state + jnp.dot(
            activation, weight_out[layer_idx], preferred_element_type=jnp.float32
        )
    return hidden_state.astype(jnp.bfloat16)


def trig_table(wave_ids, longitudes, lon_total):
    phase_angle = (wave_ids[:, None] * longitudes[None, :] % lon_total).astype(jnp.float32) * (
        2.0 * math.pi / lon_total
    )
    stacked = jnp.stack([jnp.cos(phase_angle), -jnp.sin(phase_angle)], axis=1) / math.sqrt(
        lon_total
    )
    return stacked.astype(jnp.bfloat16)


def local(
    grid_state,
    weight_in,
    bias_in,
    weight_out,
    quad_weights,
    diffusion,
    legendre,
    chan_table,
    wave_table,
):
    lat_rows, lon_cols, channels = grid_state.shape
    lat_count = lax.axis_size("lat")
    lon_count = lax.axis_size("lon")
    lon_total = lon_cols * lon_count
    per_dev = channels // lat_count
    owned_slots = legendre.shape[0]
    top_degree = legendre.shape[2]
    flat_rows = grid_state.reshape(lat_rows * lon_cols, channels)
    columns = column_layers(flat_rows, weight_in, bias_in, weight_out).reshape(
        lat_rows, lon_cols, channels
    )
    ordered = jnp.take(columns, chan_table, axis=2)
    levels = lax.all_to_all(ordered, "lat", split_axis=2, concat_axis=0, tiled=True)
    trig_all = trig_table(wave_table, jnp.arange(lon_total, dtype=jnp.int32), lon_total)
    lon_here = lax.axis_index("lon") * lon_cols + jnp.arange(lon_cols, dtype=jnp.int32)
    trig_rows = trig_table(wave_table, lon_here, lon_total)
    fourier = lax.psum_scatter(
        jnp.einsum("srj,ljk->skrl", trig_rows, levels, preferred_element_type=jnp.float32),
        "lon",
        scatter_dimension=0,
        tiled=True,
    )
    weighted = (fourier * quad_weights).astype(jnp.bfloat16)
    raw_spec = jnp.einsum("skrl,sln->skrn", weighted, legendre, preferred_element_type=jnp.float32)
    my_waves = lax.dynamic_slice_in_dim(
        wave_table, lax.axis_index("lon") * owned_slots, owned_slots, 0
    )
    degree = jnp.arange(top_degree, dtype=jnp.int32)
    triangle = (degree[None, :] >= my_waves[:, None]).astype(jnp.float32)
    my_chans = lax.dynamic_slice_in_dim(chan_table, lax.axis_index("lat") * per_dev, per_dev, 0)
    degree_f = degree.astype(jnp.float32)
    damping = (
        jnp.take(diffusion, my_chans)[:, None]
        * (degree_f * (degree_f + 1.0))[None, :]
        / float(top_degree * top_degree)
    )
    spectral = raw_spec * triangle[:, None, None, :] / (1.0 + damping)[None, :, None, :]
    back_fourier = jnp.einsum(
        "skrn,sln->skrl",
        spectral.astype(jnp.bfloat16),
        legendre,
        preferred_element_type=jnp.float32,
    ).astype(jnp.bfloat16)
    all_waves = lax.all_to_all(back_fourier, "lon", split_axis=3, concat_axis=0, tiled=True)
    band_tendency = jnp.einsum(
        "skrl,srj->ljk", all_waves, trig_all, preferred_element_type=jnp.float32
    ).astype(jnp.bfloat16)
    tendency = lax.all_to_all(
        lax.all_to_all(band_tendency, "lon", split_axis=1, concat_axis=0, tiled=True),
        "lat",
        split_axis=0,
        concat_axis=2,
        tiled=True,
    )
    tendency = jnp.take(tendency, jnp.argsort(chan_table), axis=2)
    updated = (columns.astype(jnp.float32) + tendency.astype(jnp.float32)).astype(jnp.bfloat16)
    return (updated, spectral)


def solution(mesh):
    placed = (P("lat", "lon", None), P(), P(), P(), P(), P(), P("lon", None, None), P(), P())
    return jax.shard_map(
        local,
        mesh=mesh,
        in_specs=placed,
        out_specs=(P("lat", "lon", None), P("lon", "lat", None, None)),
        check_vma=False,
    )
```

profile of v0, /device:TPU:0, one launch (start us, length us, event | category | flops | bytes accessed | tf_op | source)
XLA Modules:
  0.0 105.3 jit_solution(2320604026377320569)
XLA Ops:
  8.5 1.0 slice_reduce_fusion
  9.5 1.1 %multiply_reduce_fusion.5 = f32[15,48]{1,0:T(8,128)S(1)} fusion(bf16[15,48,128]{2,1,0:T(8,128)(2,1)} %param.11), kind=kLoop, calls=%fused_computation.121 | loop fusion | flops 275760 | bytes 187200 | tf_op jit(solution)/shard_map/reduce_sum | solution.py:11
  10.6 1.1 %multiply_convert_fusion.15 = bf16[15,48,128]{2,1,0:T(8,128)(2,1)S(1)} fusion(bf16[15,48,128]{2,1,0:T(8,128)(2,1)} %param.11, f32[15,48]{1,0:T(8,128)S(1)} %add_rsqrt_fusion), kind=kLoop, calls=%fused_computation.120 | loop fusion | flops 276480 | bytes 371520 | tf_op jit(solution)/shard_map/convert_element_type | solution.py:12
  11.7 1.9 %multiply_reduce_fusion.4 = (f32[720]{0:T(1024)S(1)}, f32[720,128]{1,0:T(8,128)S(1)}) fusion(bf16[6,384,128]{2,1,0:T(8,128)(2,1)} %param.14, bf16[720,128]{1,0:T(8,128)(2,1)S(1)} %bitcast.137, f32[384]{0:T(512)S(1)} %get-tuple-element.15, bf16[6,128,384]{2,1,0:T(8,128)(2,1)} %param.12, bf16[720,128]{1,0:T(8,128)(2,1)} %bitcast.136), kind=kOutput, calls=%fused_computation.119 | convolution fusion | flops 144690480 | bytes 938304 | tf_op jit(solution)/shard_map/dot_general | solution.py:18
  15.4 0.9 multiply_reduce_fusion.1
  19.4 1.4 %reshape.364 = bf16[8,2,5760]{2,1,0:T(2,128)(2,1)} reshape(bf16[128,15,48]{2,1,0:T(8,128)(2,1)S(1)} %fusion.193) | data formatting | bytes 368640
  20.8 5.2 %all-to-all-start = ((bf16[8,2,5760]{2,1,0:T(2,128)(2,1)}), bf16[8,2,5760]{2,1,0:T(2,128)(2,1)S(1)}, u32[]{:S(2)}, u32[]{:S(2)}) async-start(bf16[8,2,5760]{2,1,0:T(2,128)(2,1)} %reshape.364), calls=%async_computation | async-start | bytes 368640 | tf_op jit(solution)/shard_map/all_to_all | solution.py:57
  26.3 5.8 %all-to-all-done = bf16[8,2,5760]{2,1,0:T(2,128)(2,1)S(1)} async-done(((bf16[8,2,5760]{2,1,0:T(2,128)(2,1)}), bf16[8,2,5760]{2,1,0:T(2,128)(2,1)S(1)}, u32[]{:S(2)}, u32[]{:S(2)}) %all-to-all-start) | async-done | bytes 184352 | tf_op jit(solution)/shard_map/all_to_all | solution.py:57
  32.8 1.2 %convolution_bitcast_fusion.1 = f32[32,16,2,120]{3,0,2,1:T(8,128)} fusion(bf16[120,48,16,1]{1,2,0,3:T(8,128)(2,1)S(1)} %bitcast.129, f32[32,1,48]{2,0,1:T(8,128)S(1)} %get-tuple-element.18, f32[32,1,48]{2,0,1:T(8,128)S(1)} %get-tuple-element.17), kind=kOutput, calls=%fused_computation.16 | convolution fusion | flops 11805696 | bytes 688128 | tf_op jit(solution)/shard_map/srj,ljk->skrl/dot_general | solution.py:62
  35.1 20.2 %reduce-scatter.2.cloned.1.call-done = f32[8,16,2,120]{3,0,2,1:T(8,128)} async-done(((f32[32,16,2,120]{3,0,2,1:T(8,128)}), f32[8,16,2,120]{3,0,2,1:T(8,128)}) %reduce-scatter.2.cloned.1.call-update) | async-done | bytes 122896 | tf_op jit(solution)/shard_map/reduce_scatter | solution.py:61
  55.2 0.9 multiply_convert_fusion.16
  56.9 1.0 reshape.366
  58.0 3.3 %all-to-all-start.1 = ((bf16[4,2,3840]{2,1,0:T(2,128)(2,1)}), bf16[4,2,3840]{2,1,0:T(2,128)(2,1)S(1)}, u32[]{:S(2)}, u32[]{:S(2)}) async-start(bf16[4,2,3840]{2,1,0:T(2,128)(2,1)} %reshape.366), calls=%async_computation.2 | async-start | bytes 122880 | tf_op jit(solution)/shard_map/all_to_all | solution.py:88
  61.5 5.5 %all-to-all-done.1 = bf16[4,2,3840]{2,1,0:T(2,128)(2,1)S(1)} async-done(((bf16[4,2,3840]{2,1,0:T(2,128)(2,1)}), bf16[4,2,3840]{2,1,0:T(2,128)(2,1)S(1)}, u32[]{:S(2)}, u32[]{:S(2)}) %all-to-all-start.1) | async-done | bytes 61472 | tf_op jit(solution)/shard_map/all_to_all | solution.py:88
  69.2 2.1 %reshape.368 = bf16[4,2,11520]{2,1,0:T(2,128)(2,1)} reshape(bf16[192,16,30]{2,1,0:T(8,128)(2,1)S(1)} %bitcast.127) | data formatting | bytes 368640
  71.3 3.5 %all-to-all-start.2 = ((bf16[4,2,11520]{2,1,0:T(2,128)(2,1)}), bf16[4,2,11520]{2,1,0:T(2,128)(2,1)S(1)}, u32[]{:S(2)}, u32[]{:S(2)}) async-start(bf16[4,2,11520]{2,1,0:T(2,128)(2,1)} %reshape.368), calls=%async_computation.3 | async-start | bytes 368640 | tf_op jit(solution)/shard_map/all_to_all | solution.py:93
  74.8 2.5 %sort.17 = (s32[128]{0:T(128)}, s32[128]{0:T(128)S(1)}) sort(s32[128]{0:T(128)S(1)} %copy-done.4, s32[128]{0:T(128)S(1)} %iota.31), dimensions={0}, to_apply=%region_7.9 | sort | flops 896 | bytes 2048 | tf_op jit(solution)/shard_map/jit(argsort)/sort | solution.py:99
  77.4 3.4 %all-to-all-done.2 = bf16[4,2,11520]{2,1,0:T(2,128)(2,1)S(1)} async-done(((bf16[4,2,11520]{2,1,0:T(2,128)(2,1)}), bf16[4,2,11520]{2,1,0:T(2,128)(2,1)S(1)}, u32[]{:S(2)}, u32[]{:S(2)}) %all-to-all-start.2) | async-done | bytes 184352 | tf_op jit(solution)/shard_map/all_to_all | solution.py:93
  80.8 2.1 %reshape.369 = bf16[192,16,30]{2,1,0:T(8,128)(2,1)S(1)} reshape(bf16[4,2,11520]{2,1,0:T(2,128)(2,1)S(1)} %all-to-all-done.2) | data formatting | bytes 368640
  82.9 1.3 %copy.47 = bf16[30,4,48,16]{2,1,3,0:T(4,128)(2,1)S(1)} copy(bf16[30,4,48,16]{0,3,2,1:T(8,128)(2,1)S(1)} %bitcast.126) | data formatting | bytes 368640 | tf_op jit(solution)/shard_map/all_to_all | solution.py:93
  84.3 1.4 %reshape.370 = bf16[8,2,5760]{2,1,0:T(2,128)(2,1)} reshape(bf16[120,16,48]{2,1,0:T(8,128)(2,1)S(1)} %bitcast.133) | data formatting | bytes 368640
  85.7 3.7 %all-to-all-start.3 = ((bf16[8,2,5760]{2,1,0:T(2,128)(2,1)}), bf16[8,2,5760]{2,1,0:T(2,128)(2,1)S(1)}, u32[]{:S(2)}, u32[]{:S(2)}) async-start(bf16[8,2,5760]{2,1,0:T(2,128)(2,1)} %reshape.370), calls=%async_computation.4 | async-start | bytes 368640 | tf_op jit(solution)/shard_map/all_to_all | solution.py:92
  90.1 5.4 %all-to-all-done.3 = bf16[8,2,5760]{2,1,0:T(2,128)(2,1)S(1)} async-done(((bf16[8,2,5760]{2,1,0:T(2,128)(2,1)}), bf16[8,2,5760]{2,1,0:T(2,128)(2,1)S(1)}, u32[]{:S(2)}, u32[]{:S(2)}) %all-to-all-start.3) | async-done | bytes 184352 | tf_op jit(solution)/shard_map/all_to_all | solution.py:92
  97.3 1.1 %copy.39 = bf16[15,48,128]{2,1,0:T(8,128)(2,1)} copy(bf16[15,48,128]{1,0,2:T(8,128)(2,1)S(1)} %add_convert_fusion) | data formatting | bytes 368640
  (63 shorter events, 14.1 us)
Async XLA Ops:
  7.2 49.0 %copy-start = (bf16[8,120,32]{1,2,0:T(8,128)(2,1)S(1)}, bf16[8,120,32]{1,2,0:T(8,128)(2,1)}, u32[]{:S(2)}) copy-start(bf16[8,120,32]{1,2,0:T(8,128)(2,1)} %param.17) | copy-start | bytes 184324
  11.7 1.9 %copy-start.5 = (bf16[6,384,128]{2,1,0:T(8,128)(2,1)S(1)}, bf16[6,384,128]{2,1,0:T(8,128)(2,1)}, u32[]{:S(2)}) copy-start(bf16[6,384,128]{2,1,0:T(8,128)(2,1)} %param.14) | copy-start | bytes 1769476
  11.7 1.9 %copy-start.6 = (bf16[6,128,384]{2,1,0:T(8,128)(2,1)S(1)}, bf16[6,128,384]{2,1,0:T(8,128)(2,1)}, u32[]{:S(2)}) copy-start(bf16[6,128,384]{2,1,0:T(8,128)(2,1)} %param.12) | copy-start | bytes 1769476
  19.4 6.6 %copy-start.2 = (s32[32]{0:T(128)S(1)}, s32[32]{0:T(128)}, u32[]{:S(2)}) copy-start(s32[32]{0:T(128)} %param.19) | copy-start | bytes 388
  20.8 11.3 %all-to-all-start = ((bf16[8,2,5760]{2,1,0:T(2,128)(2,1)}), bf16[8,2,5760]{2,1,0:T(2,128)(2,1)S(1)}, u32[]{:S(2)}, u32[]{:S(2)}) async-start(bf16[8,2,5760]{2,1,0:T(2,128)(2,1)} %reshape.364), calls=%async_computation | async-start | bytes 368640 | tf_op jit(solution)/shard_map/all_to_all | solution.py:57
  25.9 29.3 %reduce-scatter.2.cloned.1.call-start = ((), (), s32[]{:S(2)}) async-start(), calls=%async_computation.5 | async-start | bytes 655360 | tf_op jit(solution)/shard_map/reduce_scatter | solution.py:61
  32.8 1.3 %copy-start.4 = (s32[128]{0:T(128)S(1)}, s32[128]{0:T(128)}, u32[]{:S(2)}) copy-start(s32[128]{0:T(128)} %param.18) | copy-start | bytes 1540
  32.8 1.4 %copy-start.1 = (f32[128]{0:T(128)S(1)}, f32[128]{0:T(128)}, u32[]{:S(2)}) copy-start(f32[128]{0:T(128)} %param.16) | copy-start | bytes 1540
  34.0 21.2 %copy-start.3 = (f32[120]{0:T(128)S(1)}, f32[120]{0:T(128)}, u32[]{:S(2)}) copy-start(f32[120]{0:T(128)} %param.15) | copy-start | bytes 1444
  58.0 9.0 %all-to-all-start.1 = ((bf16[4,2,3840]{2,1,0:T(2,128)(2,1)}), bf16[4,2,3840]{2,1,0:T(2,128)(2,1)S(1)}, u32[]{:S(2)}, u32[]{:S(2)}) async-start(bf16[4,2,3840]{2,1,0:T(2,128)(2,1)} %reshape.366), calls=%async_computation.2 | async-start | bytes 122880 | tf_op jit(solution)/shard_map/all_to_all | solution.py:88
  71.3 9.5 %all-to-all-start.2 = ((bf16[4,2,11520]{2,1,0:T(2,128)(2,1)}), bf16[4,2,11520]{2,1,0:T(2,128)(2,1)S(1)}, u32[]{:S(2)}, u32[]{:S(2)}) async-start(bf16[4,2,11520]{2,1,0:T(2,128)(2,1)} %reshape.368), calls=%async_computation.3 | async-start | bytes 368640 | tf_op jit(solution)/shard_map/all_to_all | solution.py:93
  85.7 9.8 %all-to-all-start.3 = ((bf16[8,2,5760]{2,1,0:T(2,128)(2,1)}), bf16[8,2,5760]{2,1,0:T(2,128)(2,1)S(1)}, u32[]{:S(2)}, u32[]{:S(2)}) async-start(bf16[8,2,5760]{2,1,0:T(2,128)(2,1)} %reshape.370), calls=%async_computation.4 | async-start | bytes 368640 | tf_op jit(solution)/shard_map/all_to_all | solution.py:92
Sparse Core Ops, SparseCore 0:
  34.2 20.9 reduce-scatter.1
where the time goes:
time: 106 us; the launch traced here: 105 us
  waiting for transfers between devices  40.2 us (38%)
  local copies, waits for them, and re-layouts  18.8 us (18%)
  starting transfers between devices  15.7 us (15%)
  between operations  14.4 us (14%)
  other arithmetic  8.25 us (8%)
  matrix products  8.02 us (8%)
    reduce_scatter x1, waiting for transfers between devices, local(): lax.psum_scatter(jnp.einsum('srj,ljk->skrl', trig_rows, levels, preferred...  20.2 us
    unnamed x24, local copies, waits for them, and re-layouts  11.4 us
    dot_general x6, matrix products, column_layers(): jnp.dot(activation, weight_out[layer_idx], preferred_element_type=jnp.flo...  6.23 us
    all_to_all x1, waiting for transfers between devices, local(): lax.all_to_all(ordered, 'lat', split_axis=2, concat_axis=0, tiled=True)  5.79 us
    all_to_all x1, waiting for transfers between devices, local(): lax.all_to_all(back_fourier, 'lon', split_axis=3, concat_axis=0, tiled=True)  5.47 us
    all_to_all x1, waiting for transfers between devices, local(): lax.all_to_all(lax.all_to_all(band_tendency, 'lon', split_axis=1, concat_...  5.36 us
    all_to_all x1, starting transfers between devices, local(): lax.all_to_all(ordered, 'lat', split_axis=2, concat_axis=0, tiled=True)  5.16 us
    all_to_all x1, starting transfers between devices, local(): lax.all_to_all(lax.all_to_all(band_tendency, 'lon', split_axis=1, concat_...  3.66 us
  transfers between devices with their start and end apart: 5, of which 5 were waited for; matrix products, arithmetic and copies ran while one was open for 4% of the time, Pallas kernels for 0%

commit v1 on v0

--- a/solution.py
+++ b/solution.py
@@ -3,6 +3,18 @@
 import jax.numpy as jnp
 from jax import lax
 from jax.sharding import PartitionSpec as P
+
+
+def cut_along(shard, dim, size):
+    shape = shard.shape
+    parts = shard.reshape(*shape[:dim], size, shape[dim] // size, *shape[dim + 1 :])
+    return jnp.moveaxis(parts, dim, 0)
+
+
+def joined_along(blocks, dim):
+    blocks = jnp.moveaxis(blocks, 0, dim)
+    dims = blocks.shape
+    return blocks.reshape(*dims[:dim], dims[dim] * dims[dim + 1], *dims[dim + 2 :])
 
 
 def column_layers(column_rows, weight_in, bias_in, weight_out):
@@ -89,13 +101,15 @@
     band_tendency = jnp.einsum(
         "skrl,srj->ljk", all_waves, trig_all, preferred_element_type=jnp.float32
     ).astype(jnp.bfloat16)
-    tendency = lax.all_to_all(
-        lax.all_to_all(band_tendency, "lon", split_axis=1, concat_axis=0, tiled=True),
-        "lat",
-        split_axis=0,
-        concat_axis=2,
-        tiled=True,
-    )
+    array = lax.all_to_all(band_tendency, "lon", split_axis=1, concat_axis=0, tiled=True)
+    count, position = (lax.axis_size("lat"), lax.axis_index("lat"))
+    blocks = cut_along(array, 0, count)
+    finished = [blocks[position]]
+    for lap in range(1, count):
+        sent = blocks[position ^ lap]
+        finished.append(lax.ppermute(sent, "lat", [(i, i ^ lap) for i in range(count)]))
+    blocks = jnp.stack(finished)[position ^ jnp.arange(count)]
+    tendency = joined_along(blocks, 2)
     tendency = jnp.take(tendency, jnp.argsort(chan_table), axis=2)
     updated = (columns.astype(jnp.float32) + tendency.astype(jnp.float32)).astype(jnp.bfloat16)
     return (updated, spectral)

time: 106 us -> 110 us (1.038)
  starting transfers between devices: 15.7 us -> 18.4 us
  waiting for transfers between devices: 40.2 us -> 41.8 us
  local copies, waits for them, and re-layouts: 18.8 us -> 17.7 us
    ppermute x0 -> x7, starting transfers between devices: none -> 6.37 us  [local(): lax.ppermute(sent, 'lat', [(i, i ^ lap) for i in range(count)])]
    all_to_all x1 -> x0, waiting for transfers between devices: 5.36 us -> none  [local(): lax.all_to_all(lax.all_to_all(band_tendency, 'lon', split_axis=1, concat_...]
    ppermute x0 -> x7, waiting for transfers between devices: none -> 4.46 us  [local(): lax.ppermute(sent, 'lat', [(i, i ^ lap) for i in range(count)])]
    all_to_all x1 -> x0, starting transfers between devices: 3.66 us -> none  [local(): lax.all_to_all(lax.all_to_all(band_tendency, 'lon', split_axis=1, concat_...]
    all_to_all x1, waiting for transfers between devices: 3.39 us -> 6.05 us  [local(): lax.all_to_all(band_tendency, 'lon', split_axis=1, concat_axis=0, tiled=T...]
    unnamed x24 -> x28, local copies, waits for them, and re-layouts: 11.4 us -> 9.56 us
  transfers between devices with their start and end apart: 5 -> 11, of which waited for: 5 -> 7; matrix products, arithmetic and copies ran while one was open for 4% -> 2% of each run, Pallas kernels for 0% -> 0%
where the time goes in v1:
time: 110 us; the launch traced here: 109 us
  waiting for transfers between devices  41.8 us (38%)
  starting transfers between devices  18.4 us (17%)
  local copies, waits for them, and re-layouts  17.7 us (16%)
  between operations  14.5 us (13%)
  other arithmetic  8.9 us (8%)
  matrix products  8 us (7%)
    reduce_scatter x1, waiting for transfers between devices, local(): lax.psum_scatter(jnp.einsum('srj,ljk->skrl', trig_rows, levels, preferred...  20.2 us
    unnamed x28, local copies, waits for them, and re-layouts  9.56 us
    ppermute x7, starting transfers between devices, local(): lax.ppermute(sent, 'lat', [(i, i ^ lap) for i in range(count)])  6.37 us
    dot_general x6, matrix products, column_layers(): jnp.dot(activation, weight_out[layer_idx], preferred_element_type=jnp.flo...  6.21 us
    all_to_all x1, waiting for transfers between devices, local(): lax.all_to_all(band_tendency, 'lon', split_axis=1, concat_axis=0, tiled=T...  6.05 us
    all_to_all x1, waiting for transfers between devices, local(): lax.all_to_all(ordered, 'lat', split_axis=2, concat_axis=0, tiled=True)  5.79 us
    all_to_all x1, waiting for transfers between devices, local(): lax.all_to_all(back_fourier, 'lon', split_axis=3, concat_axis=0, tiled=True)  5.29 us
    all_to_all x1, starting transfers between devices, local(): lax.all_to_all(ordered, 'lat', split_axis=2, concat_axis=0, tiled=True)  5.16 us
  transfers between devices with their start and end apart: 11, of which 7 were waited for; matrix products, arithmetic and copies ran while one was open for 2% of the time, Pallas kernels for 0%

profile of v1, /device:TPU:0, one launch (start us, length us, event | category | flops | bytes accessed | tf_op | source)
XLA Modules:
  0.0 109.2 jit_solution(9798807019564183767)
XLA Ops:
  7.2 3.2 %sort.17 = (s32[128]{0:T(128)}, s32[128]{0:T(128)S(1)}) sort(s32[128]{0:T(128)} %param.18, s32[128]{0:T(128)S(1)} %iota.36), dimensions={0}, to_apply=%region_7.9 | sort | flops 896 | bytes 2048 | tf_op jit(solution)/shard_map/jit(argsort)/sort | solution.py:113
  12.7 1.1 %multiply_reduce_fusion.5 = f32[15,48]{1,0:T(8,128)S(1)} fusion(bf16[15,48,128]{2,1,0:T(8,128)(2,1)} %param.11), kind=kLoop, calls=%fused_computation.122 | loop fusion | flops 275760 | bytes 187200 | tf_op jit(solution)/shard_map/reduce_sum | solution.py:23
  13.8 1.1 multiply_convert_fusion.15
  14.9 1.9 %multiply_reduce_fusion.4 = (f32[720]{0:T(1024)S(1)}, f32[720,128]{1,0:T(8,128)S(1)}) fusion(bf16[6,384,128]{2,1,0:T(8,128)(2,1)} %param.14, bf16[720,128]{1,0:T(8,128)(2,1)S(1)} %bitcast.163, f32[384]{0:T(512)S(1)} %get-tuple-element.15, bf16[6,128,384]{2,1,0:T(8,128)(2,1)} %param.12, bf16[720,128]{1,0:T(8,128)(2,1)} %bitcast.162), kind=kOutput, calls=%fused_computation.120 | convolution fusion | flops 144690480 | bytes 938304 | tf_op jit(solution)/shard_map/dot_general | solution.py:30
  22.6 1.4 %reshape.397 = bf16[8,2,5760]{2,1,0:T(2,128)(2,1)} reshape(bf16[128,15,48]{2,1,0:T(8,128)(2,1)S(1)} %fusion.194) | data formatting | bytes 368640
  23.9 5.2 %all-to-all-start = ((bf16[8,2,5760]{2,1,0:T(2,128)(2,1)}), bf16[8,2,5760]{2,1,0:T(2,128)(2,1)S(1)}, u32[]{:S(2)}, u32[]{:S(2)}) async-start(bf16[8,2,5760]{2,1,0:T(2,128)(2,1)} %reshape.397), calls=%async_computation | async-start | bytes 368640 | tf_op jit(solution)/shard_map/all_to_all | solution.py:69
  29.4 5.8 %all-to-all-done = bf16[8,2,5760]{2,1,0:T(2,128)(2,1)S(1)} async-done(((bf16[8,2,5760]{2,1,0:T(2,128)(2,1)}), bf16[8,2,5760]{2,1,0:T(2,128)(2,1)S(1)}, u32[]{:S(2)}, u32[]{:S(2)}) %all-to-all-start) | async-done | bytes 184352 | tf_op jit(solution)/shard_map/all_to_all | solution.py:69
  36.0 1.2 %convolution_bitcast_fusion.1 = f32[32,16,2,120]{3,0,2,1:T(8,128)} fusion(bf16[120,48,16,1]{1,2,0,3:T(8,128)(2,1)S(1)} %bitcast.157, f32[32,1,48]{2,0,1:T(8,128)S(1)} %get-tuple-element.26, f32[32,1,48]{2,0,1:T(8,128)S(1)} %get-tuple-element.25), kind=kOutput, calls=%fused_computation.17 | convolution fusion | flops 11805696 | bytes 688128 | tf_op jit(solution)/shard_map/srj,ljk->skrl/dot_general | solution.py:74
  38.2 20.2 %reduce-scatter.2.cloned.1.call-done = f32[8,16,2,120]{3,0,2,1:T(8,128)} async-done(((f32[32,16,2,120]{3,0,2,1:T(8,128)}), f32[8,16,2,120]{3,0,2,1:T(8,128)}) %reduce-scatter.2.cloned.1.call-update) | async-done | bytes 122896 | tf_op jit(solution)/shard_map/reduce_scatter | solution.py:73
  60.1 1.0 reshape.399
  61.1 3.5 %all-to-all-start.1 = ((bf16[4,2,3840]{2,1,0:T(2,128)(2,1)}), bf16[4,2,3840]{2,1,0:T(2,128)(2,1)S(1)}, u32[]{:S(2)}, u32[]{:S(2)}) async-start(bf16[4,2,3840]{2,1,0:T(2,128)(2,1)} %reshape.399), calls=%async_computation.2 | async-start | bytes 122880 | tf_op jit(solution)/shard_map/all_to_all | solution.py:100
  64.8 5.3 %all-to-all-done.1 = bf16[4,2,3840]{2,1,0:T(2,128)(2,1)S(1)} async-done(((bf16[4,2,3840]{2,1,0:T(2,128)(2,1)}), bf16[4,2,3840]{2,1,0:T(2,128)(2,1)S(1)}, u32[]{:S(2)}, u32[]{:S(2)}) %all-to-all-start.1) | async-done | bytes 61472 | tf_op jit(solution)/shard_map/all_to_all | solution.py:100
  72.3 2.1 %reshape.401 = bf16[4,2,11520]{2,1,0:T(2,128)(2,1)} reshape(bf16[192,16,30]{2,1,0:T(8,128)(2,1)S(1)} %bitcast.154) | data formatting | bytes 368640
  74.5 3.4 %all-to-all-start.2 = ((bf16[4,2,11520]{2,1,0:T(2,128)(2,1)}), bf16[4,2,11520]{2,1,0:T(2,128)(2,1)S(1)}, u32[]{:S(2)}, u32[]{:S(2)}) async-start(bf16[4,2,11520]{2,1,0:T(2,128)(2,1)} %reshape.401), calls=%async_computation.3 | async-start | bytes 368640 | tf_op jit(solution)/shard_map/all_to_all | solution.py:104
  77.9 6.0 %all-to-all-done.2 = bf16[4,2,11520]{2,1,0:T(2,128)(2,1)S(1)} async-done(((bf16[4,2,11520]{2,1,0:T(2,128)(2,1)}), bf16[4,2,11520]{2,1,0:T(2,128)(2,1)S(1)}, u32[]{:S(2)}, u32[]{:S(2)}) %all-to-all-start.2) | async-done | bytes 184352 | tf_op jit(solution)/shard_map/all_to_all | solution.py:104
  83.9 2.1 %reshape.402 = bf16[192,16,30]{2,1,0:T(8,128)(2,1)S(1)} reshape(bf16[4,2,11520]{2,1,0:T(2,128)(2,1)S(1)} %all-to-all-done.2) | data formatting | bytes 368640
  86.1 1.3 %copy.47 = bf16[30,4,48,16]{2,1,3,0:T(4,128)(2,1)S(1)} copy(bf16[30,4,48,16]{0,3,2,1:T(8,128)(2,1)S(1)} %bitcast.153) | data formatting | bytes 368640 | tf_op jit(solution)/shard_map/all_to_all | solution.py:104
  88.3 1.4 %collective-permute-start.1 = (bf16[15,48,16]{1,2,0:T(8,128)(2,1)S(1)}, bf16[15,48,16]{1,2,0:T(8,128)(2,1)S(1)}, u32[]{:S(2)}, u32[]{:S(2)}) collective-permute-start(bf16[15,48,16]{1,2,0:T(8,128)(2,1)S(1)} %get-tuple-element.22), channel_id=1, source_target_pairs={{0,8},{4,12},{8,0},{12,4},{16,24},{20,28},{24,16},{28,20},{1,9},{5... | collective-permute-start | bytes 69128 | tf_op jit(solution)/shard_map/ppermute | solution.py:110
  90.2 1.5 %collective-permute-start.3 = (bf16[15,48,16]{1,2,0:T(8,128)(2,1)S(1)}, bf16[15,48,16]{1,2,0:T(8,128)(2,1)S(1)}, u32[]{:S(2)}, u32[]{:S(2)}) collective-permute-start(bf16[15,48,16]{1,2,0:T(8,128)(2,1)S(1)} %get-tuple-element.20), channel_id=1, source_target_pairs={{0,16},{4,20},{8,24},{12,28},{16,0},{20,4},{24,8},{28,12},{1,17},{... | collective-permute-start | bytes 69128 | tf_op jit(solution)/shard_map/ppermute | solution.py:110
  91.8 2.4 %collective-permute-start.5 = (bf16[15,48,16]{1,2,0:T(8,128)(2,1)S(1)}, bf16[15,48,16]{1,2,0:T(8,128)(2,1)S(1)}, u32[]{:S(2)}, u32[]{:S(2)}) collective-permute-start(bf16[15,48,16]{1,2,0:T(8,128)(2,1)S(1)} %get-tuple-element.18), channel_id=1, source_target_pairs={{0,24},{4,28},{8,16},{12,20},{16,8},{20,12},{24,0},{28,4},{1,25},{... | collective-permute-start | bytes 69128 | tf_op jit(solution)/shard_map/ppermute | solution.py:110
  94.7 1.0 collective-permute-done.4
  95.8 1.5 %collective-permute-done.5 = bf16[15,48,16]{1,2,0:T(8,128)(2,1)S(1)} collective-permute-done((bf16[15,48,16]{1,2,0:T(8,128)(2,1)S(1)}, bf16[15,48,16]{1,2,0:T(8,128)(2,1)S(1)}, u32[]{:S(2)}, u32[]{:S(2)}) %collective-permute-start.5) | collective-permute-done | bytes 23072 | tf_op jit(solution)/shard_map/ppermute | solution.py:110
  97.2 2.0 %collective-permute-done.6 = bf16[15,48,16]{1,2,0:T(8,128)(2,1)S(1)} collective-permute-done((bf16[15,48,16]{1,2,0:T(8,128)(2,1)S(1)}, bf16[15,48,16]{1,2,0:T(8,128)(2,1)S(1)}, u32[]{:S(2)}, u32[]{:S(2)}) %collective-permute-start.6) | collective-permute-done | bytes 23072 | tf_op jit(solution)/shard_map/ppermute | solution.py:110
  101.3 1.1 %copy.39 = bf16[15,48,128]{2,1,0:T(8,128)(2,1)} copy(bf16[15,48,128]{1,0,2:T(8,128)(2,1)S(1)} %add_convert_fusion) | data formatting | bytes 368640
  (82 shorter events, 18.2 us)
Async XLA Ops:
  7.2 52.2 %copy-start = (bf16[8,120,32]{1,2,0:T(8,128)(2,1)S(1)}, bf16[8,120,32]{1,2,0:T(8,128)(2,1)}, u32[]{:S(2)}) copy-start(bf16[8,120,32]{1,2,0:T(8,128)(2,1)} %param.17) | copy-start | bytes 184324
  14.9 1.9 %copy-start.5 = (bf16[6,384,128]{2,1,0:T(8,128)(2,1)S(1)}, bf16[6,384,128]{2,1,0:T(8,128)(2,1)}, u32[]{:S(2)}) copy-start(bf16[6,384,128]{2,1,0:T(8,128)(2,1)} %param.14) | copy-start | bytes 1769476
  14.9 1.9 %copy-start.6 = (bf16[6,128,384]{2,1,0:T(8,128)(2,1)S(1)}, bf16[6,128,384]{2,1,0:T(8,128)(2,1)}, u32[]{:S(2)}) copy-start(bf16[6,128,384]{2,1,0:T(8,128)(2,1)} %param.12) | copy-start | bytes 1769476
  22.6 6.6 %copy-start.3 = (s32[32]{0:T(128)S(1)}, s32[32]{0:T(128)}, u32[]{:S(2)}) copy-start(s32[32]{0:T(128)} %param.19) | copy-start | bytes 388
  23.9 11.3 %all-to-all-start = ((bf16[8,2,5760]{2,1,0:T(2,128)(2,1)}), bf16[8,2,5760]{2,1,0:T(2,128)(2,1)S(1)}, u32[]{:S(2)}, u32[]{:S(2)}) async-start(bf16[8,2,5760]{2,1,0:T(2,128)(2,1)} %reshape.397), calls=%async_computation | async-start | bytes 368640 | tf_op jit(solution)/shard_map/all_to_all | solution.py:69
  29.1 29.3 %reduce-scatter.2.cloned.1.call-start = ((), (), s32[]{:S(2)}) async-start(), calls=%async_computation.4 | async-start | bytes 655360 | tf_op jit(solution)/shard_map/reduce_scatter | solution.py:73
  36.0 1.3 %copy-start.2 = (s32[128]{0:T(128)S(1)}, s32[128]{0:T(128)}, u32[]{:S(2)}) copy-start(s32[128]{0:T(128)} %param.18) | copy-start | bytes 1540
  36.0 1.4 %copy-start.1 = (f32[128]{0:T(128)S(1)}, f32[128]{0:T(128)}, u32[]{:S(2)}) copy-start(f32[128]{0:T(128)} %param.16) | copy-start | bytes 1540
  37.2 21.2 %copy-start.4 = (f32[120]{0:T(128)S(1)}, f32[120]{0:T(128)}, u32[]{:S(2)}) copy-start(f32[120]{0:T(128)} %param.15) | copy-start | bytes 1444
  61.1 9.0 %all-to-all-start.1 = ((bf16[4,2,3840]{2,1,0:T(2,128)(2,1)}), bf16[4,2,3840]{2,1,0:T(2,128)(2,1)S(1)}, u32[]{:S(2)}, u32[]{:S(2)}) async-start(bf16[4,2,3840]{2,1,0:T(2,128)(2,1)} %reshape.399), calls=%async_computation.2 | async-start | bytes 122880 | tf_op jit(solution)/shard_map/all_to_all | solution.py:100
  74.5 9.5 %all-to-all-start.2 = ((bf16[4,2,11520]{2,1,0:T(2,128)(2,1)}), bf16[4,2,11520]{2,1,0:T(2,128)(2,1)S(1)}, u32[]{:S(2)}, u32[]{:S(2)}) async-start(bf16[4,2,11520]{2,1,0:T(2,128)(2,1)} %reshape.401), calls=%async_computation.3 | async-start | bytes 368640 | tf_op jit(solution)/shard_map/all_to_all | solution.py:104
  87.5 4.3 %collective-permute-start = (bf16[15,48,16]{1,2,0:T(8,128)(2,1)S(1)}, bf16[15,48,16]{1,2,0:T(8,128)(2,1)S(1)}, u32[]{:S(2)}, u32[]{:S(2)}) collective-permute-start(bf16[15,48,16]{1,2,0:T(8,128)(2,1)S(1)} %get-tuple-element.23), channel_id=1, source_target_pairs={{0,4},{4,0},{8,12},{12,8},{16,20},{20,16},{24,28},{28,24},{1,5},{5... | collective-permute-start | bytes 69128 | tf_op jit(solution)/shard_map/ppermute | solution.py:110
  88.3 5.9 %collective-permute-start.1 = (bf16[15,48,16]{1,2,0:T(8,128)(2,1)S(1)}, bf16[15,48,16]{1,2,0:T(8,128)(2,1)S(1)}, u32[]{:S(2)}, u32[]{:S(2)}) collective-permute-start(bf16[15,48,16]{1,2,0:T(8,128)(2,1)S(1)} %get-tuple-element.22), channel_id=1, source_target_pairs={{0,8},{4,12},{8,0},{12,4},{16,24},{20,28},{24,16},{28,20},{1,9},{5... | collective-permute-start | bytes 69128 | tf_op jit(solution)/shard_map/ppermute | solution.py:110
  89.7 4.9 %collective-permute-start.2 = (bf16[15,48,16]{1,2,0:T(8,128)(2,1)S(1)}, bf16[15,48,16]{1,2,0:T(8,128)(2,1)S(1)}, u32[]{:S(2)}, u32[]{:S(2)}) collective-permute-start(bf16[15,48,16]{1,2,0:T(8,128)(2,1)S(1)} %get-tuple-element.21), channel_id=1, source_target_pairs={{0,12},{4,8},{8,4},{12,0},{16,28},{20,24},{24,20},{28,16},{1,13},{... | collective-permute-start | bytes 69128 | tf_op jit(solution)/shard_map/ppermute | solution.py:110
  90.2 4.5 %collective-permute-start.3 = (bf16[15,48,16]{1,2,0:T(8,128)(2,1)S(1)}, bf16[15,48,16]{1,2,0:T(8,128)(2,1)S(1)}, u32[]{:S(2)}, u32[]{:S(2)}) collective-permute-start(bf16[15,48,16]{1,2,0:T(8,128)(2,1)S(1)} %get-tuple-element.20), channel_id=1, source_target_pairs={{0,16},{4,20},{8,24},{12,28},{16,0},{20,4},{24,8},{28,12},{1,17},{... | collective-permute-start | bytes 69128 | tf_op jit(solution)/shard_map/ppermute | solution.py:110
  91.7 4.1 %collective-permute-start.4 = (bf16[15,48,16]{1,2,0:T(8,128)(2,1)S(1)}, bf16[15,48,16]{1,2,0:T(8,128)(2,1)S(1)}, u32[]{:S(2)}, u32[]{:S(2)}) collective-permute-start(bf16[15,48,16]{1,2,0:T(8,128)(2,1)S(1)} %get-tuple-element.19), channel_id=1, source_target_pairs={{0,20},{4,16},{8,28},{12,24},{16,4},{20,0},{24,12},{28,8},{1,21},{... | collective-permute-start | bytes 69128 | tf_op jit(solution)/shard_map/ppermute | solution.py:110
  91.8 5.4 %collective-permute-start.5 = (bf16[15,48,16]{1,2,0:T(8,128)(2,1)S(1)}, bf16[15,48,16]{1,2,0:T(8,128)(2,1)S(1)}, u32[]{:S(2)}, u32[]{:S(2)}) collective-permute-start(bf16[15,48,16]{1,2,0:T(8,128)(2,1)S(1)} %get-tuple-element.18), channel_id=1, source_target_pairs={{0,24},{4,28},{8,16},{12,20},{16,8},{20,12},{24,0},{28,4},{1,25},{... | collective-permute-start | bytes 69128 | tf_op jit(solution)/shard_map/ppermute | solution.py:110
  94.2 5.0 %collective-permute-start.6 = (bf16[15,48,16]{1,2,0:T(8,128)(2,1)S(1)}, bf16[15,48,16]{1,2,0:T(8,128)(2,1)S(1)}, u32[]{:S(2)}, u32[]{:S(2)}) collective-permute-start(bf16[15,48,16]{1,2,0:T(8,128)(2,1)S(1)} %get-tuple-element.17), channel_id=1, source_target_pairs={{0,28},{4,24},{8,20},{12,16},{16,12},{20,8},{24,4},{28,0},{1,29},{... | collective-permute-start | bytes 69128 | tf_op jit(solution)/shard_map/ppermute | solution.py:110
Sparse Core Ops, SparseCore 0:
  37.4 20.9 reduce-scatter.1
